TPU v7x, 256 devices: a whole 4x4x8 slice. The times are simulated.
256 devices in a mesh: clip: 2 (over core), ctx: 16 (over y, x), head: 8 (over z).
Axes of the slice: x: 4, y: 4, z: 8, core: 2. Of those that a mesh axis runs over, the one named last changes fastest.
Arguments:
- queries: bfloat16 [16384, 24, 128], P(('clip', 'ctx', 'head')), parts along dimension 0
- key_rows: bfloat16 [16384, 24, 128], P(('clip', 'ctx', 'head')), parts along dimension 0
- values: bfloat16 [16384, 24, 128], P(('clip', 'ctx', 'head')), parts along dimension 0, may hold values from -6 to 6
- query_tan: bfloat16 [16384, 24, 128], P(('clip', 'ctx', 'head')), parts along dimension 0, may hold values from -6 to 6
- key_tan: bfloat16 [16384, 24, 128], P(('clip', 'ctx', 'head')), parts along dimension 0, may hold values from -6 to 6
- value_tan: bfloat16 [16384, 24, 128], P(('clip', 'ctx', 'head')), parts along dimension 0, may hold values from -6 to 6
- used_tiles: int32 [32, 16, 2], P(('clip', 'ctx')), parts along dimension 0, may hold values from 0 to 3, as said below
- picked_slots: int32 [128, 8], P(('clip', 'ctx')), parts along dimension 0, may hold values from 0 to 31, as said below
- tile_count: int32 [128], P(('clip', 'ctx')), parts along dimension 0, may hold values from 4 to 8
Outputs:
- attended: bfloat16 [16384, 24, 128], P(('clip', 'ctx', 'head')), parts along dimension 0
- attended_tan: bfloat16 [16384, 24, 128], P(('clip', 'ctx', 'head')), parts along dimension 0
There are 2 independent parts, one for each index of `clip`. A program takes and returns all parts, laid end to end along the dimension named above; each array names one. Nothing has to cross between parts.
Inputs may be any that keep to these rules, and one draw needn't show every extreme that they name: `used_tiles`: for each a and c the 2 entries are different tile numbers. `picked_slots`: each row holds 8 different entries.
All inputs are finite; a program needn't handle non-finite values.
Results may differ from a plain program's by a relative error of at most 0.011.
Values may be sent and summed in bfloat16 or wider, within the bound.
No kernel may reach another device: no remote copies, remote signals or barrier semaphores. Data moves between devices by JAX's collectives and lax.ppermute only.
A program may use at most 128 MiB of HBM per device.

v0:
```python
import jax
import jax.numpy as jnp
from jax import lax
from jax.sharding import PartitionSpec as P

TILE = 128


def attend_tiles(query_blk, key_blk, value_blk, query_dir, key_dir, value_dir, live_keys):
    factor = query_blk.shape[-1] ** (-0.5)
    score = (
        jnp.einsum("bqhd,bkhd->bhqk", query_blk, key_blk, preferred_element_type=jnp.float32)
        * factor
    )
    score_dir = (
        jnp.einsum("bqhd,bkhd->bhqk", query_dir, key_blk, preferred_element_type=jnp.float32)
        + jnp.einsum("bqhd,bkhd->bhqk", query_blk, key_dir, preferred_element_type=jnp.float32)
    ) * factor
    allowed = live_keys[:, None, None, :]
    masked = jnp.where(allowed, score, -jnp.inf)
    row_max = jnp.max(masked, axis=-1, keepdims=True)
    expo = jnp.where(allowed, jnp.exp(masked - row_max), 0.0)
    prob = expo / jnp.sum(expo, axis=-1, keepdims=True)
    centre = jnp.sum(prob * score_dir, axis=-1, keepdims=True)
    prob_dir = prob * (score_dir - centre)
    prob_b = prob.astype(jnp.bfloat16)
    prob_db = prob_dir.astype(jnp.bfloat16)
    output = jnp.einsum("bhqk,bkhd->bqhd", prob_b, value_blk, preferred_element_type=jnp.float32)
    output_dir = jnp.einsum(
        "bhqk,bkhd->bqhd", prob_db, value_blk, preferred_element_type=jnp.float32
    ) + jnp.einsum("bhqk,bkhd->bqhd", prob_b, value_dir, preferred_element_type=jnp.float32)
    return (output.astype(jnp.bfloat16), output_dir.astype(jnp.bfloat16))


def body(
    queries, key_rows, values, query_tan, key_tan, value_tan, used_tiles, picked_slots, tile_count
):
    tiles_here = picked_slots.shape[0]
    slots = picked_slots.shape[1]
    capacity = used_tiles.shape[2]
    shards = lax.axis_size("ctx")
    query_h, key_h, value_h, query_dh, key_dh, value_dh = (
        lax.all_to_all(queries, "head", split_axis=1, concat_axis=0, tiled=True),
        lax.all_to_all(key_rows, "head", split_axis=1, concat_axis=0, tiled=True),
        lax.all_to_all(values, "head", split_axis=1, concat_axis=0, tiled=True),
        lax.all_to_all(query_tan, "head", split_axis=1, concat_axis=0, tiled=True),
        lax.all_to_all(key_tan, "head", split_axis=1, concat_axis=0, tiled=True),
        lax.all_to_all(value_tan, "head", split_axis=1, concat_axis=0, tiled=True),
    )
    local_heads = key_h.shape[1]
    width = key_h.shape[2]
    banks = (
        lax.all_gather(key_h, "ctx", axis=0, tiled=True),
        lax.all_gather(value_h, "ctx", axis=0, tiled=True),
        lax.all_gather(key_dh, "ctx", axis=0, tiled=True),
        lax.all_gather(value_dh, "ctx", axis=0, tiled=True),
    )
    banks = tuple(
        (part_bank.reshape(shards * tiles_here, TILE, local_heads, width) for part_bank in banks)
    )
    slot_tile = picked_slots // capacity * tiles_here + jnp.take(
        used_tiles[0].reshape(-1), picked_slots
    )
    fetched = tuple(
        (
            part_bank[slot_tile].reshape(tiles_here, slots * TILE, local_heads, width)
            for part_bank in banks
        )
    )
    live_keys = (jnp.arange(slots * TILE, dtype=jnp.int32) // TILE)[None, :] < tile_count[:, None]
    output, output_dir = attend_tiles(
        query_h.reshape(tiles_here, TILE, local_heads, width),
        fetched[0],
        fetched[1],
        query_dh.reshape(tiles_here, TILE, local_heads, width),
        fetched[2],
        fetched[3],
        live_keys,
    )
    output = output.reshape(tiles_here * TILE, local_heads, width)
    output_dir = output_dir.reshape(tiles_here * TILE, local_heads, width)
    attended, attended_tan = (
        lax.all_to_all(output, "head", split_axis=0, concat_axis=1, tiled=True),
        lax.all_to_all(output_dir, "head", split_axis=0, concat_axis=1, tiled=True),
    )
    return (attended, attended_tan)


def solution(mesh):
    placed = (
        P(("clip", "ctx", "head"), None, None),
        P(("clip", "ctx", "head"), None, None),
        P(("clip", "ctx", "head"), None, None),
        P(("clip", "ctx", "head"), None, None),
        P(("clip", "ctx", "head"), None, None),
        P(("clip", "ctx", "head"), None, None),
        P(("clip", "ctx"), None, None),
        P(("clip", "ctx"), None),
        P(("clip", "ctx")),
    )
    return jax.shard_map(
        body,
        mesh=mesh,
        in_specs=placed,
        out_specs=(P(("clip", "ctx", "head"), None, None), P(("clip", "ctx", "head"), None, None)),
        check_vma=False,
    )
```

profile of v0, /device:TPU:2, one launch (start us, length us, event | category | flops | bytes accessed | tf_op | source)
XLA Modules:
  0.0 391.8 jit_solution(16037578458585309891)
XLA Ops:
  8.4 22.9 %all_to_all.138 = bf16[64,24,128]{2,0,1:T(8,128)(2,1)S(1)} all-to-all(bf16[64,24,128]{2,0,1:T(8,128)(2,1)S(1)} %copy.125), channel_id=1, replica_groups=mesh['clip'=2,'ctx'=16,'head'=8] {'head'}, dimensions={1} | all-to-all | bytes 786432 | tf_op jit(solution)/shard_map/all_to_all | solution.py:44
  33.3 16.0 %all_to_all.139 = bf16[64,24,128]{2,0,1:T(8,128)(2,1)S(1)} all-to-all(bf16[64,24,128]{2,0,1:T(8,128)(2,1)S(1)} %copy.143), channel_id=1, replica_groups=mesh['clip'=2,'ctx'=16,'head'=8] {'head'}, dimensions={1} | all-to-all | bytes 786432 | tf_op jit(solution)/shard_map/all_to_all | solution.py:47
  51.2 15.5 %all_to_all.140 = bf16[64,24,128]{2,0,1:T(8,128)(2,1)S(1)} all-to-all(bf16[64,24,128]{2,0,1:T(8,128)(2,1)S(1)} %copy.120), channel_id=1, replica_groups=mesh['clip'=2,'ctx'=16,'head'=8] {'head'}, dimensions={1} | all-to-all | bytes 786432 | tf_op jit(solution)/shard_map/all_to_all | solution.py:45
  67.7 14.3 %all_to_all.141 = bf16[64,24,128]{2,0,1:T(8,128)(2,1)S(1)} all-to-all(bf16[64,24,128]{2,0,1:T(8,128)(2,1)S(1)} %copy.151), channel_id=1, replica_groups=mesh['clip'=2,'ctx'=16,'head'=8] {'head'}, dimensions={1} | all-to-all | bytes 786432 | tf_op jit(solution)/shard_map/all_to_all | solution.py:48
  83.6 3.5 all-to-all-start.2
  88.1 10.8 %all-to-all-done.2 = bf16[64,24,128]{2,0,1:T(8,128)(2,1)S(1)} async-done(((bf16[64,24,128]{2,0,1:T(8,128)(2,1)}), bf16[64,24,128]{2,0,1:T(8,128)(2,1)S(1)}, u32[]{:S(2)}, u32[]{:S(2)}) %all-to-all-start.2) | async-done | bytes 393248 | tf_op jit(solution)/shard_map/all_to_all | solution.py:43
  98.9 3.5 all-to-all-start.4
  104.3 9.8 %all-to-all-done.4 = bf16[64,24,128]{2,0,1:T(8,128)(2,1)S(1)} async-done(((bf16[64,24,128]{2,0,1:T(8,128)(2,1)}), bf16[64,24,128]{2,0,1:T(8,128)(2,1)S(1)}, u32[]{:S(2)}, u32[]{:S(2)}) %all-to-all-start.4) | async-done | bytes 393248 | tf_op jit(solution)/shard_map/all_to_all | solution.py:46
  114.2 8.2 %copy.127 = bf16[64,128,3,128]{3,1,2,0:T(8,128)(2,1)} copy(bf16[64,128,3,128]{3,1,0,2:T(8,128)(2,1)} %bitcast.71) | data formatting | bytes 12582912 | tf_op jit(solution)/shard_map/reshape | solution.py:59
  122.4 3.9 %gather_fusion.2 = bf16[32,128,3,128]{3,1,2,0:T(8,128)(2,1)S(1)} fusion(bf16[64,128,3,128]{3,1,2,0:T(8,128)(2,1)} %copy.127, s32[1024]{0:T(1024)S(1)} %pad_clamp_fusion), kind=kCustom, calls=%fused_computation.2 | custom fusion | bytes 6291584 | tf_op jit(solution)/shard_map/gather | solution.py:66
  126.3 1.9 copy.128
  128.3 35.3 %all-gather.9.cloned.1.call-done = bf16[8192,3,128]{2,0,1:T(8,128)(2,1)} async-done(((bf16[512,3,128]{2,0,1:T(8,128)(2,1)}), bf16[8192,3,128]{2,0,1:T(8,128)(2,1)}) %all-gather.9.cloned.1.call-update) | async-done | bytes 6291472 | tf_op jit(solution)/shard_map/all_gather | solution.py:55
  163.6 8.1 %copy.145 = bf16[64,128,3,128]{3,1,2,0:T(8,128)(2,1)} copy(bf16[64,128,3,128]{3,1,0,2:T(8,128)(2,1)} %bitcast.72) | data formatting | bytes 12582912 | tf_op jit(solution)/shard_map/reshape | solution.py:59
  171.6 3.9 %gather_fusion.3 = bf16[32,128,3,128]{3,1,2,0:T(8,128)(2,1)S(1)} fusion(bf16[64,128,3,128]{3,1,2,0:T(8,128)(2,1)} %copy.145, s32[1024]{0:T(1024)S(1)} %pad_clamp_fusion), kind=kCustom, calls=%fused_computation.3 | custom fusion | bytes 6291584 | tf_op jit(solution)/shard_map/gather | solution.py:66
  175.6 1.9 copy.146
  177.5 55.2 %all-gather.5.cloned.1.call-done = bf16[8192,3,128]{2,0,1:T(8,128)(2,1)} async-done(((bf16[512,3,128]{2,0,1:T(8,128)(2,1)}), bf16[8192,3,128]{2,0,1:T(8,128)(2,1)}) %all-gather.5.cloned.1.call-update) | async-done | bytes 6291472 | tf_op jit(solution)/shard_map/all_gather | solution.py:54
  232.7 8.0 %copy.123 = bf16[64,128,3,128]{3,1,2,0:T(8,128)(2,1)} copy(bf16[64,128,3,128]{3,1,0,2:T(8,128)(2,1)} %bitcast.73) | data formatting | bytes 12582912 | tf_op jit(solution)/shard_map/reshape | solution.py:59
  240.8 3.9 %gather_fusion.1 = bf16[32,128,3,128]{3,1,2,0:T(8,128)(2,1)S(1)} fusion(bf16[64,128,3,128]{3,1,2,0:T(8,128)(2,1)} %copy.123, s32[1024]{0:T(1024)S(1)} %pad_clamp_fusion), kind=kCustom, calls=%fused_computation.1 | custom fusion | bytes 6291584 | tf_op jit(solution)/shard_map/gather | solution.py:66
  244.7 1.9 copy.124
  246.6 54.6 %all-gather.11.cloned.1.call-done = bf16[8192,3,128]{2,0,1:T(8,128)(2,1)} async-done(((bf16[512,3,128]{2,0,1:T(8,128)(2,1)}), bf16[8192,3,128]{2,0,1:T(8,128)(2,1)}) %all-gather.11.cloned.1.call-update) | async-done | bytes 6291472 | tf_op jit(solution)/shard_map/all_gather | solution.py:56
  301.2 8.0 %copy.153 = bf16[64,128,3,128]{3,1,2,0:T(8,128)(2,1)} copy(bf16[64,128,3,128]{3,1,0,2:T(8,128)(2,1)} %bitcast.74) | data formatting | bytes 12582912 | tf_op jit(solution)/shard_map/reshape | solution.py:59
  309.2 3.9 %gather_fusion.4 = bf16[32,128,3,128]{3,1,2,0:T(8,128)(2,1)S(1)} fusion(bf16[64,128,3,128]{3,1,2,0:T(8,128)(2,1)} %copy.153, s32[1024]{0:T(1024)S(1)} %pad_clamp_fusion), kind=kCustom, calls=%fused_computation.4 | custom fusion | bytes 6291584 | tf_op jit(solution)/shard_map/gather | solution.py:66
  313.2 1.9 copy.154
  316.2 3.6 fusion.29
  319.8 5.9 %fusion.77 = (f32[4,3,128]{2,1,0:T(4,128)S(1)}, f32[4,3,128,1024]{2,3,1,0:T(8,128)}) fusion(pred[4,1024]{1,0:T(4,128)(4,1)S(1)} %broadcast_compare_fusion, bf16[4,1024,3,128]{3,1,0,2:T(8,128)(2,1)S(1)} %bitcast.70, bf16[4,128,3,128]{3,1,0,2:T(8,128)(2,1)} %bitcast.96), kind=kOutput, calls=%fused_computation.71 | convolution fusion | flops 410518528 | bytes 9840640 | tf_op jit(solution)/shard_map/sub | solution.py:22
  325.7 6.9 %fusion.1 = (f32[4,3,128]{2,1,0:T(4,128)S(1)}, f32[4,3,1024,128]{3,2,1,0:T(8,128)S(1)}) fusion(f32[4,3,128,1024]{2,3,1,0:T(8,128)} %get-tuple-element.11, f32[4,3,128]{2,1,0:T(4,128)S(1)} %get-tuple-element.10, f32[4,3,1024,128]{3,2,1,0:T(8,128)} %fusion.29, bf16[4,128,3,128]{3,1,0,2:T(8,128)(2,1)S(1)} %bitcast.97, bf16[4,1024,3,128]{3,1,0,2:T(8,128)(2,1)} %bitcast.77), kind=kOutput, calls=%fused_computation.8 | convolution fusion | flops 410515968 | bytes 22425600 | tf_op jit(solution)/shard_map/bqhd,bkhd->bhqk/dot_general | solution.py:17
  333.9 1.8 fusion.11
  338.2 7.0 %all-to-all-start.7 = ((bf16[512,3,128]{2,1,0:T(4,128)(2,1)}), bf16[512,3,128]{2,1,0:T(4,128)(2,1)}, u32[]{:S(2)}, u32[]{:S(2)}) async-start(bf16[512,3,128]{2,1,0:T(4,128)(2,1)} %copy.158), calls=%async_computation.7 | async-start | bytes 1048576 | tf_op jit(solution)/shard_map/all_to_all | solution.py:84
  345.2 3.9 fusion.52
  350.2 12.5 %all-to-all-done.7 = bf16[512,3,128]{2,1,0:T(4,128)(2,1)} async-done(((bf16[512,3,128]{2,1,0:T(4,128)(2,1)}), bf16[512,3,128]{2,1,0:T(4,128)(2,1)}, u32[]{:S(2)}, u32[]{:S(2)}) %all-to-all-start.7) | async-done | bytes 393248 | tf_op jit(solution)/shard_map/all_to_all | solution.py:84
  362.8 3.5 all-to-all-start.3
  368.4 15.7 %all-to-all-done.3 = bf16[512,3,128]{2,1,0:T(4,128)(2,1)S(1)} async-done(((bf16[512,3,128]{2,1,0:T(4,128)(2,1)}), bf16[512,3,128]{2,1,0:T(4,128)(2,1)S(1)}, u32[]{:S(2)}, u32[]{:S(2)}) %all-to-all-start.3) | async-done | bytes 393248 | tf_op jit(solution)/shard_map/all_to_all | solution.py:83
  (68 shorter events, 19.8 us)
Async XLA Ops:
  7.2 60.4 %copy-start.4 = (bf16[64,24,128]{2,1,0:T(8,128)(2,1)S(1)}, bf16[64,24,128]{2,1,0:T(8,128)(2,1)}, u32[]{:S(2)}) copy-start(bf16[64,24,128]{2,1,0:T(8,128)(2,1)} %param.14) | copy-start | bytes 1179652
  7.2 75.6 %copy-start.5 = (bf16[64,24,128]{2,1,0:T(8,128)(2,1)S(1)}, bf16[64,24,128]{2,1,0:T(8,128)(2,1)}, u32[]{:S(2)}) copy-start(bf16[64,24,128]{2,1,0:T(8,128)(2,1)} %param.9) | copy-start | bytes 1179652
  7.2 79.9 %copy-start.8 = (s32[4,8]{1,0:T(4,128)S(1)}, s32[4,8]{1,0:T(4,128)}, u32[]{:S(2)}) copy-start(s32[4,8]{1,0:T(4,128)} %param.16) | copy-start | bytes 388
  7.2 80.0 %copy-start.6 = (bf16[64,24,128]{2,1,0:T(8,128)(2,1)S(1)}, bf16[64,24,128]{2,1,0:T(8,128)(2,1)}, u32[]{:S(2)}) copy-start(bf16[64,24,128]{2,1,0:T(8,128)(2,1)} %param.12) | copy-start | bytes 1179652
  7.2 107.0 %all-gather.7.cloned.1.call-start = ((), (), s32[]{:S(2)}) async-start(), calls=%async_computation.9 | async-start | bytes 6684672 | tf_op jit(solution)/shard_map/all_gather | solution.py:53
  31.4 71.0 %copy-start.9 = (s32[1,16,2]{1,2,0:T(2,128)S(1)}, s32[1,16,2]{1,2,0:T(2,128)}, u32[]{:S(2)}) copy-start(s32[1,16,2]{1,2,0:T(2,128)} %param.15) | copy-start | bytes 388
  32.2 131.4 %all-gather.9.cloned.1.call-start = ((), (), s32[]{:S(2)}) async-start(), calls=%async_computation.10 | async-start | bytes 6684672 | tf_op jit(solution)/shard_map/all_gather | solution.py:55
  33.3 70.1 %copy-start.10 = (s32[4]{0:T(128)S(1)}, s32[4]{0:T(128)}, u32[]{:S(2)}) copy-start(s32[4]{0:T(128)} %param.17) | copy-start | bytes 52
  50.1 182.7 %all-gather.5.cloned.1.call-start = ((), (), s32[]{:S(2)}) async-start(), calls=%async_computation.8 | async-start | bytes 6684672 | tf_op jit(solution)/shard_map/all_gather | solution.py:54
  67.5 233.7 %all-gather.11.cloned.1.call-start = ((), (), s32[]{:S(2)}) async-start(), calls=%async_computation.11 | async-start | bytes 6684672 | tf_op jit(solution)/shard_map/all_gather | solution.py:56
  83.6 15.3 %all-to-all-start.2 = ((bf16[64,24,128]{2,0,1:T(8,128)(2,1)}), bf16[64,24,128]{2,0,1:T(8,128)(2,1)S(1)}, u32[]{:S(2)}, u32[]{:S(2)}) async-start(bf16[64,24,128]{2,0,1:T(8,128)(2,1)} %copy.129), calls=%async_computation.2 | async-start | bytes 786432 | tf_op jit(solution)/shard_map/all_to_all | solution.py:43
  98.9 15.3 %all-to-all-start.4 = ((bf16[64,24,128]{2,0,1:T(8,128)(2,1)}), bf16[64,24,128]{2,0,1:T(8,128)(2,1)S(1)}, u32[]{:S(2)}, u32[]{:S(2)}) async-start(bf16[64,24,128]{2,0,1:T(8,128)(2,1)} %copy.139), calls=%async_computation.4 | async-start | bytes 786432 | tf_op jit(solution)/shard_map/all_to_all | solution.py:46
  313.2 3.0 copy-start
  315.0 4.7 %copy-start.1 = (bf16[32,128,3,128]{3,1,0,2:T(8,128)(2,1)S(1)}, bf16[32,128,3,128]{3,1,0,2:T(8,128)(2,1)}, u32[]{:S(2)}) copy-start(bf16[32,128,3,128]{3,1,0,2:T(8,128)(2,1)} %copy.128) | copy-start | bytes 9437188
  319.8 5.9 %copy-start.7 = (bf16[8,64,3,128]{3,1,0,2:T(8,128)(2,1)S(1)}, bf16[8,64,3,128]{3,1,0,2:T(8,128)(2,1)}, u32[]{:S(2)}) copy-start(bf16[8,64,3,128]{3,1,0,2:T(8,128)(2,1)} %copy.130) | copy-start | bytes 1179652
  325.7 7.0 %copy-start.2 = (bf16[32,128,3,128]{3,1,0,2:T(8,128)(2,1)S(1)}, bf16[32,128,3,128]{3,1,0,2:T(8,128)(2,1)}, u32[]{:S(2)}) copy-start(bf16[32,128,3,128]{3,1,0,2:T(8,128)(2,1)} %copy.124) | copy-start | bytes 9437188
  325.7 8.2 %copy-start.11 = (f32[4,3,128,1024]{2,3,1,0:T(8,128)S(1)}, f32[4,3,128,1024]{2,3,1,0:T(8,128)}, u32[]{:S(2)}) copy-start(f32[4,3,128,1024]{2,3,1,0:T(8,128)} %get-tuple-element.11) | copy-start | bytes 18874372
  333.9 1.9 copy-start.3
  338.2 24.6 %all-to-all-start.7 = ((bf16[512,3,128]{2,1,0:T(4,128)(2,1)}), bf16[512,3,128]{2,1,0:T(4,128)(2,1)}, u32[]{:S(2)}, u32[]{:S(2)}) async-start(bf16[512,3,128]{2,1,0:T(4,128)(2,1)} %copy.158), calls=%async_computation.7 | async-start | bytes 1048576 | tf_op jit(solution)/shard_map/all_to_all | solution.py:84
  362.8 21.4 %all-to-all-start.3 = ((bf16[512,3,128]{2,1,0:T(4,128)(2,1)}), bf16[512,3,128]{2,1,0:T(4,128)(2,1)S(1)}, u32[]{:S(2)}, u32[]{:S(2)}) async-start(bf16[512,3,128]{2,1,0:T(4,128)(2,1)} %copy.136), calls=%async_computation.3 | async-start | bytes 1048576 | tf_op jit(solution)/shard_map/all_to_all | solution.py:83
Sparse Core Ops, SparseCore 0:
  32.3 62.6 all-gather.6
  97.4 66.0 all-gather.8
  166.6 66.0 all-gather.4
  235.0 66.0 all-gather.10
where the time goes:
time: 394 us; the launch traced here: 392 us
  waiting for transfers between devices  194 us (49%)
  local copies, waits for them, and re-layouts  74 us (19%)
  blocking collectives  68.7 us (17%)
  matrix products  23.3 us (6%)
  starting transfers between devices  17.6 us (4%)
  between operations  14.1 us (4%)
    all_gather x1, waiting for transfers between devices, body(): lax.all_gather(value_h, 'ctx', axis=0, tiled=True)  55.2 us
    all_gather x1, waiting for transfers between devices, body(): lax.all_gather(value_dh, 'ctx', axis=0, tiled=True)  54.6 us
    all_gather x1, waiting for transfers between devices, body(): lax.all_gather(key_dh, 'ctx', axis=0, tiled=True)  35.3 us
    reshape x4, local copies, waits for them, and re-layouts, body(): part_bank.reshape(shards * tiles_here, TILE, local_heads, width)  32.3 us
    gather x8, local copies, waits for them, and re-layouts, body(): part_bank[slot_tile].reshape(tiles_here, slots * TILE, local_heads, width)  23.4 us
    all_to_all x1, blocking collectives, body(): lax.all_to_all(key_rows, 'head', split_axis=1, concat_axis=0, tiled=True)  22.9 us
    all_to_all x1, blocking collectives, body(): lax.all_to_all(key_tan, 'head', split_axis=1, concat_axis=0, tiled=True)  16 us
    all_to_all x1, waiting for transfers between devices, body(): lax.all_to_all(output, 'head', split_axis=0, concat_axis=1, tiled=True)  15.7 us
  transfers between devices with their start and end apart: 8, of which 7 were waited for; matrix products, arithmetic and copies ran while one was open for 15% of the time, Pallas kernels for 0%

commit v1 on v0

v1 whole, which is shorter than its diff:
```python
import functools

import jax
import jax.numpy as jnp
from jax import lax
from jax.experimental import pallas as pl
from jax.experimental.pallas import tpu as pltpu
from jax.sharding import Mesh, PartitionSpec as P

TILE = 128
ROW = 4
GROUP = 4
LOWEST = -3.0e38
LOG2E = 1.4426950408889634
STAT_ROWS = 16


def shift(count, step):
    return [(i, (i + step) % count) for i in range(count)]


def tile_of(block):
    return block.reshape(block.shape[0] * block.shape[1], block.shape[2])


def dot_nt(left, right):
    return lax.dot_general(
        left, right, (((1,), (1,)), ((), ())), preferred_element_type=jnp.float32
    )


def dot_nn(left, right):
    return jnp.dot(left, right, preferred_element_type=jnp.float32)


def one_pair(query, query_dir, key, key_dir, value, value_dir):
    factor = query.shape[-1] ** (-0.5)
    score = dot_nt(query, key) * (factor * LOG2E)
    score_dir = (
        dot_nt(
            jnp.concatenate([query_dir, query], axis=1), jnp.concatenate([key, key_dir], axis=1)
        )
        * factor
    )
    top = jnp.max(score, axis=1, keepdims=True)
    expo = jnp.exp2(score - top)
    total = jnp.sum(expo, axis=1, keepdims=True)
    centre = jnp.sum(expo * score_dir, axis=1, keepdims=True) / total
    expo_b = expo.astype(jnp.bfloat16)
    expo_db = (expo * (score_dir - centre)).astype(jnp.bfloat16)
    out = dot_nn(expo_b, value)
    out_dir = dot_nn(
        jnp.concatenate([expo_db, expo_b], axis=1), jnp.concatenate([value, value_dir], axis=0)
    )
    return top, total, centre, out, out_dir


def three_parts(number):
    first = number.astype(jnp.bfloat16).astype(jnp.float32)
    rest = number - first
    second = rest.astype(jnp.bfloat16).astype(jnp.float32)
    return first, second, rest - second


def attend_kernel(pairs, *refs):
    key_in, query_in, out_refs = refs[:ROW], refs[ROW : 2 * ROW], refs[2 * ROW : 3 * ROW]
    keys, queries, acc, acc_dir, tops, totals, centres, sem_k, sem_q = refs[3 * ROW :]
    copies = []
    for r in range(ROW):
        copies.append(pltpu.make_async_copy(key_in[r], keys.at[r], sem_k.at[r]))
        copies.append(pltpu.make_async_copy(query_in[r], queries.at[r], sem_q.at[r]))
    for copy in copies:
        copy.start()
    acc[...] = jnp.zeros_like(acc)
    acc_dir[...] = jnp.zeros_like(acc_dir)
    tops[...] = jnp.full_like(tops, LOWEST)
    totals[...] = jnp.zeros_like(totals)
    centres[...] = jnp.zeros_like(centres)
    for copy in copies:
        copy.wait()
    count = pairs[pairs.shape[0] - 1]

    def group(step, carry):
        codes = [pairs[step * GROUP + i] for i in range(GROUP)]
        results = []
        for code in codes:
            key_at, query_at = code & 15, (code >> 4) & 15
            key_block, key_rows = key_at >> 2, pl.ds((key_at & 3) * 2, 2)
            query_block, query_rows = query_at >> 2, pl.ds((query_at & 3) * 2, 2)
            results.append(
                one_pair(
                    tile_of(queries[query_block, query_rows, 0]),
                    tile_of(queries[query_block, query_rows, 1]),
                    tile_of(keys[key_block, key_rows, 0]),
                    tile_of(keys[key_block, key_rows, 1]),
                    tile_of(keys[key_block, key_rows, 2]),
                    tile_of(keys[key_block, key_rows, 3]),
                )
            )
        for code, (top, total, centre, out, out_dir) in zip(codes, results):
            at = code >> 8
            top_0, total_0, centre_0 = tops[at], totals[at], centres[at]
            out_0, out_dir_0 = acc[at], acc_dir[at]
            top_n = jnp.maximum(top, top_0)
            weight_0 = jnp.exp2(top_0 - top_n)
            weight = jnp.exp2(top - top_n)
            part_0, part = weight_0 * total_0, weight * total
            total_n = part_0 + part
            centre_n = (part_0 * centre_0 + part * centre) / total_n
            tops[at], totals[at], centres[at] = top_n, total_n, centre_n
            acc[at] = weight_0 * out_0 + weight * out
            acc_dir[at] = (
                weight_0 * out_dir_0
                + weight * out_dir
                + (weight_0 * (centre_0 - centre_n)) * out_0
                + (weight * (centre - centre_n)) * out
            )
        return carry

    lax.fori_loop(0, (count + GROUP - 1) // GROUP, group, 0)

    lane = lax.broadcasted_iota(jnp.int32, (TILE, TILE), 1)
    for r in range(ROW):

        def finish(t, carry, r=r):
            at = r * ROW + t
            total = totals[at]
            some = total > 0
            inverse = jnp.where(some, 1.0 / jnp.where(some, total, 1.0), 0.0)
            level = jnp.where(some, tops[at] + jnp.log2(jnp.where(some, total, 1.0)), LOWEST)
            out_refs[r][t, 0:TILE] = (acc[at] * inverse).astype(jnp.bfloat16)
            out_refs[r][t, TILE : 2 * TILE] = (acc_dir[at] * inverse).astype(jnp.bfloat16)
            table = jnp.zeros((TILE, TILE), jnp.float32)
            for column, part in enumerate(three_parts(level) + three_parts(centres[at])):
                table = jnp.where(lane == column, part, table)
            table = jnp.transpose(table, (1, 0))
            out_refs[r][t, 2 * TILE :] = table[:STAT_ROWS].astype(jnp.bfloat16)
            return carry

        lax.fori_loop(0, ROW, finish, 0)


def attend(pairs, key_blocks, query_blocks):
    width = key_blocks[0].shape[-1]
    tiles = key_blocks[0].shape[0] // 2
    rows = 2 * TILE + STAT_ROWS
    slots = ROW * tiles + 1
    anywhere = pl.BlockSpec(memory_space=pl.ANY)
    return pl.pallas_call(
        attend_kernel,
        out_shape=[jax.ShapeDtypeStruct((tiles, rows, width), jnp.bfloat16)] * ROW,
        in_specs=[pl.BlockSpec(memory_space=pltpu.SMEM)] + [anywhere] * (2 * ROW),
        out_specs=[pl.BlockSpec(memory_space=pltpu.VMEM)] * ROW,
        scratch_shapes=[
            pltpu.VMEM((ROW,) + key_blocks[0].shape, jnp.bfloat16),
            pltpu.VMEM((ROW,) + query_blocks[0].shape, jnp.bfloat16),
            pltpu.VMEM((slots, TILE, width), jnp.float32),
            pltpu.VMEM((slots, TILE, width), jnp.float32),
            pltpu.VMEM((slots, TILE, 1), jnp.float32),
            pltpu.VMEM((slots, TILE, 1), jnp.float32),
            pltpu.VMEM((slots, TILE, 1), jnp.float32),
            pltpu.SemaphoreType.DMA((ROW,)),
            pltpu.SemaphoreType.DMA((ROW,)),
        ],
        compiler_params=pltpu.CompilerParams(vmem_limit_bytes=32 * 1024 * 1024),
        cost_estimate=pl.CostEstimate(
            flops=5_000_000_000, bytes_accessed=5_000_000, transcendentals=500_000
        ),
        name="attend",
    )(pairs, *key_blocks, *query_blocks)


def combine_kernel(*refs):
    parts, out_ref = refs[:ROW], refs[ROW]
    tiles = parts[0].shape[0]

    def one_tile(t, carry):
        levels, centres = [], []
        for part in parts:
            table = part[t, 2 * TILE :].astype(jnp.float32)
            table = jnp.transpose(
                jnp.concatenate(
                    [table, jnp.zeros((TILE - STAT_ROWS, TILE), jnp.float32)], axis=0
                ),
                (1, 0),
            )
            levels.append(table[:, 0:1] + table[:, 1:2] + table[:, 2:3])
            centres.append(table[:, 3:4] + table[:, 4:5] + table[:, 5:6])
        top = functools.reduce(jnp.maximum, levels)
        weights = [jnp.exp2(level - top) for level in levels]
        inverse = 1.0 / sum(weights)
        weights = [weight * inverse for weight in weights]
        centre = sum(weight * each for weight, each in zip(weights, centres))
        out = jnp.zeros((TILE, parts[0].shape[2]), jnp.float32)
        out_dir = jnp.zeros_like(out)
        for part, weight, each in zip(parts, weights, centres):
            value = part[t, 0:TILE].astype(jnp.float32)
            value_dir = part[t, TILE : 2 * TILE].astype(jnp.float32)
            out = out + weight * value
            out_dir = out_dir + weight * value_dir + (weight * (each - centre)) * value
        half = TILE // 2
        out_ref[pl.ds(2 * t, 2), 0] = out.reshape(2, half, -1).astype(jnp.bfloat16)
        out_ref[pl.ds(2 * t, 2), 1] = out_dir.reshape(2, half, -1).astype(jnp.bfloat16)
        return carry

    lax.fori_loop(0, tiles, one_tile, 0)


def combine(parts):
    tiles, _, width = parts[0].shape
    return pl.pallas_call(
        combine_kernel,
        out_shape=jax.ShapeDtypeStruct((2 * tiles, 2, TILE // 2, width), jnp.bfloat16),
        in_specs=[pl.BlockSpec(memory_space=pltpu.VMEM)] * ROW,
        out_specs=pl.BlockSpec(memory_space=pltpu.VMEM),
        compiler_params=pltpu.CompilerParams(vmem_limit_bytes=16 * 1024 * 1024),
        cost_estimate=pl.CostEstimate(
            flops=1_000_000, bytes_accessed=1_500_000, transcendentals=1000
        ),
        name="combine",
    )(*parts)


def list_pairs(used_tiles, picked_slots, tile_count):
    row, column = lax.axis_index("cy"), lax.axis_index("cx")
    tiles, slots = picked_slots.shape
    capacity = used_tiles.shape[2]
    flat = used_tiles.reshape(-1)
    chosen = picked_slots[..., None] == jnp.arange(flat.shape[0], dtype=jnp.int32)
    tile = jnp.sum(jnp.where(chosen, flat, 0), axis=-1)
    live = jnp.arange(slots, dtype=jnp.int32)[None, :] < tile_count[:, None]
    code = jnp.where(live, picked_slots // capacity * tiles + tile, -1)
    codes = jnp.concatenate(
        [code] + [lax.ppermute(code, "cx", shift(ROW, r)) for r in range(1, ROW)], axis=0
    ).reshape(-1)
    shard = codes // tiles
    valid = (codes >= 0) & (shard % ROW == column)
    key_at = (row - shard // ROW) % ROW * tiles + codes % tiles
    size = codes.shape[0]
    query_at = jnp.arange(size, dtype=jnp.int32) // slots
    entry = (query_at * 16 + query_at) * 16 + key_at
    place = jnp.arange(size, dtype=jnp.int32)
    before = jnp.sum((place[None, :] < place[:, None]) & valid[None, :], axis=1, dtype=jnp.int32)
    wanted = jnp.arange(size + GROUP, dtype=jnp.int32)
    hit = valid[None, :] & (before[None, :] == wanted[:, None])
    count = jnp.sum(valid, dtype=jnp.int32)
    listed = jnp.where(
        wanted < count, jnp.sum(jnp.where(hit, entry[None, :], 0), axis=1), ROW * tiles * 256
    )
    return jnp.concatenate([listed, count[None]])


def body(
    queries, key_rows, values, query_tan, key_tan, value_tan, used_tiles, picked_slots, tile_count
):
    groups = lax.axis_size("head")
    tokens, heads, width = queries.shape
    per_group = heads // groups
    pairs = list_pairs(used_tiles, picked_slots, tile_count)
    stacked = jnp.stack([key_rows, key_tan, values, value_tan, queries, query_tan])
    stacked = stacked.reshape(6, tokens, groups, per_group, width).transpose(3, 2, 0, 1, 4)
    finished = []
    for h in range(per_group):
        moved = lax.all_to_all(stacked[h], "head", split_axis=0, concat_axis=0, tiled=True)
        key_part, query_part = moved[:, :4], moved[:, 4:]
        key_blocks = [key_part] + [
            lax.ppermute(key_part, "cy", shift(ROW, r)) for r in range(1, ROW)
        ]
        query_blocks = [query_part] + [
            lax.ppermute(query_part, "cx", shift(ROW, r)) for r in range(1, ROW)
        ]
        parts = attend(pairs, key_blocks, query_blocks)
        parts = [parts[0]] + [
            lax.ppermute(parts[r], "cx", shift(ROW, -r)) for r in range(1, ROW)
        ]
        whole = combine(parts)
        finished.append(
            lax.all_to_all(whole, "head", split_axis=0, concat_axis=0, tiled=True)
        )
    finished = jnp.stack(finished)
    finished = finished.transpose(2, 3, 1, 0, 4).reshape(2, tokens, heads, width)
    return finished[0], finished[1]


def solution(mesh):
    fine = Mesh(
        mesh.devices.reshape(mesh.devices.shape[0], ROW, ROW, mesh.devices.shape[2]),
        ("clip", "cy", "cx", "head"),
    )
    tokens = P(("clip", "cy", "cx", "head"), None, None)
    shards = ("clip", "cy", "cx")
    return jax.shard_map(
        body,
        mesh=fine,
        in_specs=(tokens,) * 6 + (P(shards, None, None), P(shards, None), P(shards)),
        out_specs=(tokens, tokens),
        check_vma=False,
    )
```

time: 394 us -> 242 us (0.61)
  waiting for transfers between devices: 194 us -> 39.7 us
  local copies, waits for them, and re-layouts: 74 us -> 17.7 us
  Pallas kernels: 0 us -> 56 us
  starting transfers between devices: 17.6 us -> 72.5 us
  matrix products: 23.3 us -> 0 us
  blocking collectives: 68.7 us -> 48.9 us
  between operations: 14.1 us -> 1.13 us
    all_gather x4 -> x0, waiting for transfers between devices: 145 us -> none  [the longest x1 55.2 us: body(): lax.all_gather(value_h, 'ctx', axis=0, tiled=True)]
    pallas_call x0 -> x6, Pallas kernels: none -> 56 us  [the longest x3 46 us: attend(): pl.pallas_call(attend_kernel, out_shape=[jax.ShapeDtypeStruct((tiles, row...]
    ppermute x0 -> x30, starting transfers between devices: none -> 52.7 us  [the longest x9 17.7 us: body(): lax.ppermute(key_part, 'cy', shift(ROW, r))]
    reshape x6 -> x2, local copies, waits for them, and re-layouts: 34.6 us -> 0.17 us  [the longest x1 0.09 us: list_pairs(): flat = used_tiles.reshape(-1)]
    all_to_all x4, waiting for transfers between devices: 48.9 us -> 23.5 us  [the longest x2 21.4 us: body(): lax.all_to_all(stacked[h], 'head', split_axis=0, concat_axis=0, tiled=True)]
    gather x10 -> x0, local copies, waits for them, and re-layouts: 24.2 us -> none  [the longest x8 23.4 us: body(): part_bank[slot_tile].reshape(tiles_here, slots * TILE, local_heads, width)]
    all_to_all x4 -> x2, blocking collectives: 68.7 us -> 48.9 us  [the longest x1 31.5 us: body(): lax.all_to_all(stacked[h], 'head', split_axis=0, concat_axis=0, tiled=True)]
    dot_general x5 -> x0, matrix products: 17.4 us -> none  [the longest x1 6.94 us: attend_tiles(): jnp.einsum('bqhd,bkhd->bhqk', query_blk, key_dir, preferred_element_type=...]
  transfers between devices with their start and end apart: 8 -> 34, of which waited for: 7 -> 8; matrix products, arithmetic and copies ran while one was open for 15% -> 3% of each run, Pallas kernels for 0% -> 23%
where the time goes in v1:
time: 242 us; the launch traced here: 240 us
  starting transfers between devices  72.5 us (30%)
  Pallas kernels  56 us (23%)
  blocking collectives  48.9 us (20%)
  waiting for transfers between devices  39.7 us (16%)
  local copies, waits for them, and re-layouts  17.7 us (7%)
  other arithmetic  3.69 us (2%)
    pallas_call x3, Pallas kernels, attend(): pl.pallas_call(attend_kernel, out_shape=[jax.ShapeDtypeStruct((tiles, row...  46 us
    all_to_all x1, blocking collectives, body(): lax.all_to_all(stacked[h], 'head', split_axis=0, concat_axis=0, tiled=True)  31.5 us
    all_to_all x2, waiting for transfers between devices, body(): lax.all_to_all(stacked[h], 'head', split_axis=0, concat_axis=0, tiled=True)  21.4 us
    ppermute x9, starting transfers between devices, body(): lax.ppermute(key_part, 'cy', shift(ROW, r))  17.7 us
    all_to_all x1, blocking collectives, body(): lax.all_to_all(whole, 'head', split_axis=0, concat_axis=0, tiled=True)  17.4 us
    ppermute x9, starting transfers between devices, body(): lax.ppermute(parts[r], 'cx', shift(ROW, -r))  15.7 us
    ppermute x9, starting transfers between devices, body(): lax.ppermute(query_part, 'cx', shift(ROW, r))  14.6 us
    all_to_all x2, starting transfers between devices, body(): lax.all_to_all(whole, 'head', split_axis=0, concat_axis=0, tiled=True)  12.1 us
  transfers between devices with their start and end apart: 34, of which 8 were waited for; matrix products, arithmetic and copies ran while one was open for 3% of the time, Pallas kernels for 23%

profile of v1, /device:TPU:2, one launch (start us, length us, event | category | flops | bytes accessed | tf_op | source)
XLA Modules:
  0.0 239.7 jit_solution(491271888055991997)
XLA Ops:
  4.4 1.7 slice_bitcast_fusion.2
  6.0 31.5 %all_to_all.30 = bf16[8,6,64,128]{3,2,1,0:T(8,128)(2,1)S(1)} all-to-all(bf16[8,6,64,128]{3,2,1,0:T(8,128)(2,1)S(1)} %get-tuple-element.32), channel_id=1, replica_groups=mesh['clip'=2,'cy'=4,'cx'=4,'head'=8] {'head'}, dimensions={0} | all-to-all | bytes 1572864 | tf_op jit(solution)/shard_map/all_to_all | solution.py:264
  37.5 3.5 %all-to-all-start.2 = ((bf16[8,6,64,128]{3,2,1,0:T(8,128)(2,1)}), bf16[8,6,64,128]{3,2,1,0:T(8,128)(2,1)S(1)}, u32[]{:S(2)}, u32[]{:S(2)}) async-start(bf16[8,6,64,128]{3,2,1,0:T(8,128)(2,1)} %get-tuple-element.34), calls=%async_computation.2 | async-start | bytes 1572864 | tf_op jit(solution)/shard_map/all_to_all | solution.py:264
  41.3 21.4 %all-to-all-done.2 = bf16[8,6,64,128]{3,2,1,0:T(8,128)(2,1)S(1)} async-done(((bf16[8,6,64,128]{3,2,1,0:T(8,128)(2,1)}), bf16[8,6,64,128]{3,2,1,0:T(8,128)(2,1)S(1)}, u32[]{:S(2)}, u32[]{:S(2)}) %all-to-all-start.2) | async-done | bytes 786464 | tf_op jit(solution)/shard_map/all_to_all | solution.py:264
  62.6 4.2 %all-to-all-start.4 = ((bf16[8,6,64,128]{3,2,1,0:T(8,128)(2,1)}), bf16[8,6,64,128]{3,2,1,0:T(8,128)(2,1)}, u32[]{:S(2)}, u32[]{:S(2)}) async-start(bf16[8,6,64,128]{3,2,1,0:T(8,128)(2,1)} %get-tuple-element.33), calls=%async_computation.4 | async-start | bytes 1572864 | tf_op jit(solution)/shard_map/all_to_all | solution.py:264
  69.8 2.2 collective-permute-start.2
  71.9 1.8 collective-permute-done.1
  76.0 2.5 %collective-permute-start.7 = (bf16[8,2,64,128]{3,2,1,0:T(8,128)(2,1)S(1)}, bf16[8,2,64,128]{3,2,1,0:T(8,128)(2,1)S(1)}, u32[]{:S(2)}, u32[]{:S(2)}) collective-permute-start(bf16[8,2,64,128]{3,2,1,0:T(8,128)(2,1)S(1)} %slice.48.refs_4_), channel_id=1, source_target_pairs={{0,16},{8,24},{16,0},{24,8},{1,17},{9,25},{17,1},{25,9},{2,18},{10... | collective-permute-start | bytes 786440 | tf_op jit(solution)/shard_map/ppermute | solution.py:270
  78.5 1.7 collective-permute-start.3
  80.2 3.0 %collective-permute-start.4 = (bf16[8,4,64,128]{3,2,1,0:T(8,128)(2,1)S(1)}, bf16[8,4,64,128]{3,2,1,0:T(8,128)(2,1)S(1)}, u32[]{:S(2)}, u32[]{:S(2)}) collective-permute-start(bf16[8,4,64,128]{3,2,1,0:T(8,128)(2,1)S(1)} %slice.47.refs_0_), channel_id=1, source_target_pairs={{0,64},{32,96},{64,0},{96,32},{1,65},{33,97},{65,1},{97,33},{2,66}... | collective-permute-start | bytes 1572872 | tf_op jit(solution)/shard_map/ppermute | solution.py:267
  86.3 2.0 collective-permute-start.8
  90.3 2.5 %collective-permute-done.8.refs_7_ = bf16[8,2,64,128]{3,2,1,0:T(8,128)(2,1)S(1)} collective-permute-done((bf16[8,2,64,128]{3,2,1,0:T(8,128)(2,1)S(1)}, bf16[8,2,64,128]{3,2,1,0:T(8,128)(2,1)S(1)}, u32[]{:S(2)}, u32[]{:S(2)}) %collective-permute-start.8) | collective-permute-done | bytes 262176 | tf_op jit(solution)/shard_map/ppermute | solution.py:270
  95.6 3.7 %collective-permute-start.13 = (bf16[8,4,64,128]{3,2,1,0:T(8,128)(2,1)S(1)}, bf16[8,4,64,128]{3,2,1,0:T(8,128)(2,1)}, u32[]{:S(2)}, u32[]{:S(2)}) collective-permute-start(bf16[8,4,64,128]{3,2,1,0:T(8,128)(2,1)S(1)} %slice.50.refs_0_), channel_id=1, source_target_pairs={{0,64},{32,96},{64,0},{96,32},{1,65},{33,97},{65,1},{97,33},{2,66}... | collective-permute-start | bytes 1572872 | tf_op jit(solution)/shard_map/ppermute | solution.py:267
  102.0 5.1 %collective-permute-done.4.refs_2_ = bf16[8,4,64,128]{3,2,1,0:T(8,128)(2,1)S(1)} collective-permute-done((bf16[8,4,64,128]{3,2,1,0:T(8,128)(2,1)S(1)}, bf16[8,4,64,128]{3,2,1,0:T(8,128)(2,1)S(1)}, u32[]{:S(2)}, u32[]{:S(2)}) %collective-permute-start.4) | collective-permute-done | bytes 524320 | tf_op jit(solution)/shard_map/ppermute | solution.py:267
  112.6 15.1 %attend.3 = (bf16[4,272,128]{2,1,0:T(8,128)(2,1)S(1)}, bf16[4,272,128]{2,1,0:T(8,128)(2,1)S(1)}, bf16[4,272,128]{2,1,0:T(8,128)(2,1)S(1)}, bf16[4,272,128]{2,1,0:T(8,128)(2,1)S(1)}) custom-call(s32[133]{0:T(256)S(1)} %pad_add_fusion.1.pairs, bf16[8,4,64,128]{3,2,1,0:T(8,128)(2,1)S(1)} %slice.47.refs_0_, ...), custom_call_target="tpu_custom_call" | custom-call | flops 5000000000 | bytes 5000000 | tf_op jit(solution)/shard_map/attend/pallas_call | solution.py:149
  128.7 3.3 %collective-permute-start.10 = (bf16[4,272,128]{2,1,0:T(8,128)(2,1)S(1)}, bf16[4,272,128]{2,1,0:T(8,128)(2,1)S(1)}, u32[]{:S(2)}, u32[]{:S(2)}) collective-permute-start(bf16[4,272,128]{2,1,0:T(8,128)(2,1)S(1)} %get-tuple-element.16), channel_id=1, source_target_pairs={{0,16},{8,24},{16,0},{24,8},{1,17},{9,25},{17,1},{25,9},{2,18},{10... | collective-permute-start | bytes 835592 | tf_op jit(solution)/shard_map/ppermute | solution.py:274
  132.0 2.0 collective-permute-start.9
  134.0 15.9 %attend.4 = (bf16[4,272,128]{2,1,0:T(8,128)(2,1)S(1)}, bf16[4,272,128]{2,1,0:T(8,128)(2,1)S(1)}, bf16[4,272,128]{2,1,0:T(8,128)(2,1)}, bf16[4,272,128]{2,1,0:T(8,128)(2,1)}) custom-call(s32[133]{0:T(256)S(1)} %pad_add_fusion.1.pairs, bf16[8,4,64,128]{3,2,1,0:T(8,128)(2,1)S(1)} %slice.50.refs_0_, bf16[8,4,64,128]{3,2,1,0:T(8,128)(2,1)S(1)} %collective-permute-done.12.refs_1_, ...), custom_call_target="tpu_custom_call" | custom-call | flops 5000000000 | bytes 5000000 | tf_op jit(solution)/shard_map/attend/pallas_call | solution.py:149
  149.9 2.1 collective-permute-start.18
  154.8 5.6 %collective-permute-start.22 = (bf16[8,4,64,128]{3,2,1,0:T(8,128)(2,1)S(1)}, bf16[8,4,64,128]{3,2,1,0:T(8,128)(2,1)S(1)}, u32[]{:S(2)}, u32[]{:S(2)}) collective-permute-start(bf16[8,4,64,128]{3,2,1,0:T(8,128)(2,1)S(1)} %slice.53.refs_0_), channel_id=1, source_target_pairs={{0,64},{32,96},{64,0},{96,32},{1,65},{33,97},{65,1},{97,33},{2,66}... | collective-permute-start | bytes 1572872 | tf_op jit(solution)/shard_map/ppermute | solution.py:267
  161.0 3.6 %combine.3 = bf16[8,2,64,128]{3,2,1,0:T(8,128)(2,1)} custom-call(bf16[4,272,128]{2,1,0:T(8,128)(2,1)S(1)} %get-tuple-element.14.refs_0_, bf16[4,272,128]{2,1,0:T(8,128)(2,1)S(1)} %collective-permute-done.9.refs_1_, bf16[4,272,128]{2,1,0:T(8,128)(2,1)S(1)} %collective-permute-done.10.refs_2_, bf16[4,272,128]{2,1,0:T(8,128)(2,1)S(1)} %collective-permute-done.11.refs_3_), custom_call_target="tpu_custom_call" | custom-call | flops 1000000 | bytes 1500000 | tf_op jit(solution)/shard_map/combine/pallas_call | solution.py:211
  164.5 7.1 %all-to-all-start.1 = ((bf16[8,2,64,128]{3,2,1,0:T(8,128)(2,1)}), bf16[8,2,64,128]{3,2,1,0:T(8,128)(2,1)}, u32[]{:S(2)}, u32[]{:S(2)}) async-start(bf16[8,2,64,128]{3,2,1,0:T(8,128)(2,1)} %combine.3), calls=%async_computation.1 | async-start | bytes 524288 | tf_op jit(solution)/shard_map/all_to_all | solution.py:278
  171.6 5.0 %collective-permute-start.25 = (bf16[8,2,64,128]{3,2,1,0:T(8,128)(2,1)S(1)}, bf16[8,2,64,128]{3,2,1,0:T(8,128)(2,1)}, u32[]{:S(2)}, u32[]{:S(2)}) collective-permute-start(bf16[8,2,64,128]{3,2,1,0:T(8,128)(2,1)S(1)} %slice.54.refs_4_), channel_id=1, source_target_pairs={{0,16},{8,24},{16,0},{24,8},{1,17},{9,25},{17,1},{25,9},{2,18},{10... | collective-permute-start | bytes 786440 | tf_op jit(solution)/shard_map/ppermute | solution.py:270
  176.7 3.6 %combine.4 = bf16[8,2,64,128]{3,2,1,0:T(8,128)(2,1)} custom-call(bf16[4,272,128]{2,1,0:T(8,128)(2,1)S(1)} %get-tuple-element.18.refs_0_, bf16[4,272,128]{2,1,0:T(8,128)(2,1)S(1)} %collective-permute-done.18.refs_1_, bf16[4,272,128]{2,1,0:T(8,128)(2,1)S(1)} %collective-permute-done.19.refs_2_, bf16[4,272,128]{2,1,0:T(8,128)(2,1)S(1)} %collective-permute-done.20.refs_3_), custom_call_target="tpu_custom_call" | custom-call | flops 1000000 | bytes 1500000 | tf_op jit(solution)/shard_map/combine/pallas_call | solution.py:211
  180.3 2.1 all-to-all-done.1
  182.3 5.0 %all-to-all-start.3 = ((bf16[8,2,64,128]{3,2,1,0:T(8,128)(2,1)}), bf16[8,2,64,128]{3,2,1,0:T(8,128)(2,1)}, u32[]{:S(2)}, u32[]{:S(2)}) async-start(bf16[8,2,64,128]{3,2,1,0:T(8,128)(2,1)} %combine.4), calls=%async_computation.3 | async-start | bytes 524288 | tf_op jit(solution)/shard_map/all_to_all | solution.py:278
  188.4 15.0 %attend.5 = (bf16[4,272,128]{2,1,0:T(8,128)(2,1)S(1)}, bf16[4,272,128]{2,1,0:T(8,128)(2,1)S(1)}, bf16[4,272,128]{2,1,0:T(8,128)(2,1)S(1)}, bf16[4,272,128]{2,1,0:T(8,128)(2,1)S(1)}) custom-call(s32[133]{0:T(256)S(1)} %pad_add_fusion.1.pairs, bf16[8,4,64,128]{3,2,1,0:T(8,128)(2,1)S(1)} %slice.53.refs_0_, ...), custom_call_target="tpu_custom_call" | custom-call | flops 5000000000 | bytes 5000000 | tf_op jit(solution)/shard_map/attend/pallas_call | solution.py:149
  205.0 2.6 %collective-permute-start.28 = (bf16[4,272,128]{2,1,0:T(8,128)(2,1)S(1)}, bf16[4,272,128]{2,1,0:T(8,128)(2,1)S(1)}, u32[]{:S(2)}, u32[]{:S(2)}) collective-permute-start(bf16[4,272,128]{2,1,0:T(8,128)(2,1)S(1)} %get-tuple-element.24), channel_id=1, source_target_pairs={{0,16},{8,24},{16,0},{24,8},{1,17},{9,25},{17,1},{25,9},{2,18},{10... | collective-permute-start | bytes 835592 | tf_op jit(solution)/shard_map/ppermute | solution.py:274
  207.6 2.5 %collective-permute-start.29 = (bf16[4,272,128]{2,1,0:T(8,128)(2,1)S(1)}, bf16[4,272,128]{2,1,0:T(8,128)(2,1)S(1)}, u32[]{:S(2)}, u32[]{:S(2)}) collective-permute-start(bf16[4,272,128]{2,1,0:T(8,128)(2,1)S(1)} %get-tuple-element.25), channel_id=1, source_target_pairs={{0,8},{8,16},{16,24},{24,0},{1,9},{9,17},{17,25},{25,1},{2,10},{10... | collective-permute-start | bytes 835592 | tf_op jit(solution)/shard_map/ppermute | solution.py:274
  210.1 4.9 %collective-permute-done.28.refs_2_ = bf16[4,272,128]{2,1,0:T(8,128)(2,1)S(1)} collective-permute-done((bf16[4,272,128]{2,1,0:T(8,128)(2,1)S(1)}, bf16[4,272,128]{2,1,0:T(8,128)(2,1)S(1)}, u32[]{:S(2)}, u32[]{:S(2)}) %collective-permute-start.28) | collective-permute-done | bytes 278560 | tf_op jit(solution)/shard_map/ppermute | solution.py:274
  216.2 2.9 %combine.5 = bf16[8,2,64,128]{3,2,1,0:T(8,128)(2,1)S(1)} custom-call(bf16[4,272,128]{2,1,0:T(8,128)(2,1)S(1)} %get-tuple-element.22.refs_0_, bf16[4,272,128]{2,1,0:T(8,128)(2,1)S(1)} %collective-permute-done.27.refs_1_, bf16[4,272,128]{2,1,0:T(8,128)(2,1)S(1)} %collective-permute-done.28.refs_2_, bf16[4,272,128]{2,1,0:T(8,128)(2,1)S(1)} %collective-permute-done.29.refs_3_), custom_call_target="tpu_custom_call" | custom-call | flops 1000000 | bytes 1500000 | tf_op jit(solution)/shard_map/combine/pallas_call | solution.py:211
  219.1 17.4 %all_to_all.31 = bf16[8,2,64,128]{3,2,1,0:T(8,128)(2,1)S(1)} all-to-all(bf16[8,2,64,128]{3,2,1,0:T(8,128)(2,1)S(1)} %combine.5), channel_id=1, replica_groups=mesh['clip'=2,'cy'=4,'cx'=4,'head'=8] {'head'}, dimensions={0} | all-to-all | bytes 524288 | tf_op jit(solution)/shard_map/all_to_all | solution.py:278
  (118 shorter events, 36.2 us)
Async XLA Ops:
  37.5 25.1 %all-to-all-start.2 = ((bf16[8,6,64,128]{3,2,1,0:T(8,128)(2,1)}), bf16[8,6,64,128]{3,2,1,0:T(8,128)(2,1)S(1)}, u32[]{:S(2)}, u32[]{:S(2)}) async-start(bf16[8,6,64,128]{3,2,1,0:T(8,128)(2,1)} %get-tuple-element.34), calls=%async_computation.2 | async-start | bytes 1572864 | tf_op jit(solution)/shard_map/all_to_all | solution.py:264
  62.6 38.4 %all-to-all-start.4 = ((bf16[8,6,64,128]{3,2,1,0:T(8,128)(2,1)}), bf16[8,6,64,128]{3,2,1,0:T(8,128)(2,1)}, u32[]{:S(2)}, u32[]{:S(2)}) async-start(bf16[8,6,64,128]{3,2,1,0:T(8,128)(2,1)} %get-tuple-element.33), calls=%async_computation.4 | async-start | bytes 1572864 | tf_op jit(solution)/shard_map/all_to_all | solution.py:264
  68.7 5.1 %collective-permute-start.1 = (s32[4,8]{1,0:T(4,128)S(1)}, s32[4,8]{1,0:T(4,128)S(1)}, u32[]{:S(2)}, u32[]{:S(2)}) collective-permute-start(s32[4,8]{1,0:T(4,128)S(1)} %fusion.10), channel_id=1, source_target_pairs={{0,16},{8,24},{16,0},{24,8},{1,17},{9,25},{17,1},{25,9},{2,18},{10... | collective-permute-start | bytes 392 | tf_op jit(solution)/shard_map/ppermute | solution.py:234
  74.6 11.0 %collective-permute-start.6 = (bf16[8,2,64,128]{3,2,1,0:T(8,128)(2,1)S(1)}, bf16[8,2,64,128]{3,2,1,0:T(8,128)(2,1)S(1)}, u32[]{:S(2)}, u32[]{:S(2)}) collective-permute-start(bf16[8,2,64,128]{3,2,1,0:T(8,128)(2,1)S(1)} %slice.48.refs_4_), channel_id=1, source_target_pairs={{0,8},{8,16},{16,24},{24,0},{1,9},{9,17},{17,25},{25,1},{2,10},{10... | collective-permute-start | bytes 786440 | tf_op jit(solution)/shard_map/ppermute | solution.py:270
  76.0 12.4 %collective-permute-start.7 = (bf16[8,2,64,128]{3,2,1,0:T(8,128)(2,1)S(1)}, bf16[8,2,64,128]{3,2,1,0:T(8,128)(2,1)S(1)}, u32[]{:S(2)}, u32[]{:S(2)}) collective-permute-start(bf16[8,2,64,128]{3,2,1,0:T(8,128)(2,1)S(1)} %slice.48.refs_4_), channel_id=1, source_target_pairs={{0,16},{8,24},{16,0},{24,8},{1,17},{9,25},{17,1},{25,9},{2,18},{10... | collective-permute-start | bytes 786440 | tf_op jit(solution)/shard_map/ppermute | solution.py:270
  78.5 20.8 %collective-permute-start.3 = (bf16[8,4,64,128]{3,2,1,0:T(8,128)(2,1)S(1)}, bf16[8,4,64,128]{3,2,1,0:T(8,128)(2,1)S(1)}, u32[]{:S(2)}, u32[]{:S(2)}) collective-permute-start(bf16[8,4,64,128]{3,2,1,0:T(8,128)(2,1)S(1)} %slice.47.refs_0_), channel_id=1, source_target_pairs={{0,32},{32,64},{64,96},{96,0},{1,33},{33,65},{65,97},{97,1},{2,34}... | collective-permute-start | bytes 1572872 | tf_op jit(solution)/shard_map/ppermute | solution.py:267
  80.2 27.0 %collective-permute-start.4 = (bf16[8,4,64,128]{3,2,1,0:T(8,128)(2,1)S(1)}, bf16[8,4,64,128]{3,2,1,0:T(8,128)(2,1)S(1)}, u32[]{:S(2)}, u32[]{:S(2)}) collective-permute-start(bf16[8,4,64,128]{3,2,1,0:T(8,128)(2,1)S(1)} %slice.47.refs_0_), channel_id=1, source_target_pairs={{0,64},{32,96},{64,0},{96,32},{1,65},{33,97},{65,1},{97,33},{2,66}... | collective-permute-start | bytes 1572872 | tf_op jit(solution)/shard_map/ppermute | solution.py:267
  83.2 25.0 %collective-permute-start.5 = (bf16[8,4,64,128]{3,2,1,0:T(8,128)(2,1)S(1)}, bf16[8,4,64,128]{3,2,1,0:T(8,128)(2,1)}, u32[]{:S(2)}, u32[]{:S(2)}) collective-permute-start(bf16[8,4,64,128]{3,2,1,0:T(8,128)(2,1)S(1)} %slice.47.refs_0_), channel_id=1, source_target_pairs={{0,96},{32,0},{64,32},{96,64},{1,97},{33,1},{65,33},{97,65},{2,98}... | collective-permute-start | bytes 1572872 | tf_op jit(solution)/shard_map/ppermute | solution.py:267
  86.3 6.4 %collective-permute-start.8 = (bf16[8,2,64,128]{3,2,1,0:T(8,128)(2,1)S(1)}, bf16[8,2,64,128]{3,2,1,0:T(8,128)(2,1)S(1)}, u32[]{:S(2)}, u32[]{:S(2)}) collective-permute-start(bf16[8,2,64,128]{3,2,1,0:T(8,128)(2,1)S(1)} %slice.48.refs_4_), channel_id=1, source_target_pairs={{0,24},{8,0},{16,8},{24,16},{1,25},{9,1},{17,9},{25,17},{2,26},{10... | collective-permute-start | bytes 786440 | tf_op jit(solution)/shard_map/ppermute | solution.py:270
  88.4 6.5 %collective-permute-start.15 = (bf16[8,2,64,128]{3,2,1,0:T(8,128)(2,1)S(1)}, bf16[8,2,64,128]{3,2,1,0:T(8,128)(2,1)S(1)}, u32[]{:S(2)}, u32[]{:S(2)}) collective-permute-start(bf16[8,2,64,128]{3,2,1,0:T(8,128)(2,1)S(1)} %slice.51.refs_4_), channel_id=1, source_target_pairs={{0,8},{8,16},{16,24},{24,0},{1,9},{9,17},{17,25},{25,1},{2,10},{10... | collective-permute-start | bytes 786440 | tf_op jit(solution)/shard_map/ppermute | solution.py:270
  93.4 38.5 %collective-permute-start.12 = (bf16[8,4,64,128]{3,2,1,0:T(8,128)(2,1)S(1)}, bf16[8,4,64,128]{3,2,1,0:T(8,128)(2,1)S(1)}, u32[]{:S(2)}, u32[]{:S(2)}) collective-permute-start(bf16[8,4,64,128]{3,2,1,0:T(8,128)(2,1)S(1)} %slice.50.refs_0_), channel_id=1, source_target_pairs={{0,32},{32,64},{64,96},{96,0},{1,33},{33,65},{65,97},{97,1},{2,34}... | collective-permute-start | bytes 1572872 | tf_op jit(solution)/shard_map/ppermute | solution.py:267
  95.6 36.4 %collective-permute-start.13 = (bf16[8,4,64,128]{3,2,1,0:T(8,128)(2,1)S(1)}, bf16[8,4,64,128]{3,2,1,0:T(8,128)(2,1)}, u32[]{:S(2)}, u32[]{:S(2)}) collective-permute-start(bf16[8,4,64,128]{3,2,1,0:T(8,128)(2,1)S(1)} %slice.50.refs_0_), channel_id=1, source_target_pairs={{0,64},{32,96},{64,0},{96,32},{1,65},{33,97},{65,1},{97,33},{2,66}... | collective-permute-start | bytes 1572872 | tf_op jit(solution)/shard_map/ppermute | solution.py:267
  99.3 34.7 %collective-permute-start.14 = (bf16[8,4,64,128]{3,2,1,0:T(8,128)(2,1)S(1)}, bf16[8,4,64,128]{3,2,1,0:T(8,128)(2,1)}, u32[]{:S(2)}, u32[]{:S(2)}) collective-permute-start(bf16[8,4,64,128]{3,2,1,0:T(8,128)(2,1)S(1)} %slice.50.refs_0_), channel_id=1, source_target_pairs={{0,96},{32,0},{64,32},{96,64},{1,97},{33,1},{65,33},{97,65},{2,98}... | collective-permute-start | bytes 1572872 | tf_op jit(solution)/shard_map/ppermute | solution.py:267
  107.2 20.5 %collective-permute-start.16 = (bf16[8,2,64,128]{3,2,1,0:T(8,128)(2,1)S(1)}, bf16[8,2,64,128]{3,2,1,0:T(8,128)(2,1)S(1)}, u32[]{:S(2)}, u32[]{:S(2)}) collective-permute-start(bf16[8,2,64,128]{3,2,1,0:T(8,128)(2,1)S(1)} %slice.51.refs_4_), channel_id=1, source_target_pairs={{0,16},{8,24},{16,0},{24,8},{1,17},{9,25},{17,1},{25,9},{2,18},{10... | collective-permute-start | bytes 786440 | tf_op jit(solution)/shard_map/ppermute | solution.py:270
  108.2 20.5 %collective-permute-start.17 = (bf16[8,2,64,128]{3,2,1,0:T(8,128)(2,1)S(1)}, bf16[8,2,64,128]{3,2,1,0:T(8,128)(2,1)S(1)}, u32[]{:S(2)}, u32[]{:S(2)}) collective-permute-start(bf16[8,2,64,128]{3,2,1,0:T(8,128)(2,1)S(1)} %slice.51.refs_4_), channel_id=1, source_target_pairs={{0,24},{8,0},{16,8},{24,16},{1,25},{9,1},{17,9},{25,17},{2,26},{10... | collective-permute-start | bytes 786440 | tf_op jit(solution)/shard_map/ppermute | solution.py:270
  127.7 24.3 %collective-permute-start.24 = (bf16[8,2,64,128]{3,2,1,0:T(8,128)(2,1)S(1)}, bf16[8,2,64,128]{3,2,1,0:T(8,128)(2,1)S(1)}, u32[]{:S(2)}, u32[]{:S(2)}) collective-permute-start(bf16[8,2,64,128]{3,2,1,0:T(8,128)(2,1)S(1)} %slice.54.refs_4_), channel_id=1, source_target_pairs={{0,8},{8,16},{16,24},{24,0},{1,9},{9,17},{17,25},{25,1},{2,10},{10... | collective-permute-start | bytes 786440 | tf_op jit(solution)/shard_map/ppermute | solution.py:270
  128.7 23.3 %collective-permute-start.10 = (bf16[4,272,128]{2,1,0:T(8,128)(2,1)S(1)}, bf16[4,272,128]{2,1,0:T(8,128)(2,1)S(1)}, u32[]{:S(2)}, u32[]{:S(2)}) collective-permute-start(bf16[4,272,128]{2,1,0:T(8,128)(2,1)S(1)} %get-tuple-element.16), channel_id=1, source_target_pairs={{0,16},{8,24},{16,0},{24,8},{1,17},{9,25},{17,1},{25,9},{2,18},{10... | collective-permute-start | bytes 835592 | tf_op jit(solution)/shard_map/ppermute | solution.py:274
  132.0 22.7 %collective-permute-start.11 = (bf16[4,272,128]{2,1,0:T(8,128)(2,1)S(1)}, bf16[4,272,128]{2,1,0:T(8,128)(2,1)S(1)}, u32[]{:S(2)}, u32[]{:S(2)}) collective-permute-start(bf16[4,272,128]{2,1,0:T(8,128)(2,1)S(1)} %get-tuple-element.17), channel_id=1, source_target_pairs={{0,8},{8,16},{16,24},{24,0},{1,9},{9,17},{17,25},{25,1},{2,10},{10... | collective-permute-start | bytes 835592 | tf_op jit(solution)/shard_map/ppermute | solution.py:274
  132.0 22.8 %collective-permute-start.9 = (bf16[4,272,128]{2,1,0:T(8,128)(2,1)S(1)}, bf16[4,272,128]{2,1,0:T(8,128)(2,1)S(1)}, u32[]{:S(2)}, u32[]{:S(2)}) collective-permute-start(bf16[4,272,128]{2,1,0:T(8,128)(2,1)S(1)} %get-tuple-element.15), channel_id=1, source_target_pairs={{0,24},{8,0},{16,8},{24,16},{1,25},{9,1},{17,9},{25,17},{2,26},{10... | collective-permute-start | bytes 835592 | tf_op jit(solution)/shard_map/ppermute | solution.py:274
  149.9 10.5 %collective-permute-start.18 = (bf16[4,272,128]{2,1,0:T(8,128)(2,1)S(1)}, bf16[4,272,128]{2,1,0:T(8,128)(2,1)S(1)}, u32[]{:S(2)}, u32[]{:S(2)}) collective-permute-start(bf16[4,272,128]{2,1,0:T(8,128)(2,1)S(1)} %get-tuple-element.19), channel_id=1, source_target_pairs={{0,24},{8,0},{16,8},{24,16},{1,25},{9,1},{17,9},{25,17},{2,26},{10... | collective-permute-start | bytes 835592 | tf_op jit(solution)/shard_map/ppermute | solution.py:274
  152.0 19.6 %collective-permute-start.19 = (bf16[4,272,128]{2,1,0:T(8,128)(2,1)}, bf16[4,272,128]{2,1,0:T(8,128)(2,1)S(1)}, u32[]{:S(2)}, u32[]{:S(2)}) collective-permute-start(bf16[4,272,128]{2,1,0:T(8,128)(2,1)} %get-tuple-element.20), channel_id=1, source_target_pairs={{0,16},{8,24},{16,0},{24,8},{1,17},{9,25},{17,1},{25,9},{2,18},{10... | collective-permute-start | bytes 835592 | tf_op jit(solution)/shard_map/ppermute | solution.py:274
  152.0 24.6 %collective-permute-start.20 = (bf16[4,272,128]{2,1,0:T(8,128)(2,1)}, bf16[4,272,128]{2,1,0:T(8,128)(2,1)S(1)}, u32[]{:S(2)}, u32[]{:S(2)}) collective-permute-start(bf16[4,272,128]{2,1,0:T(8,128)(2,1)} %get-tuple-element.21), channel_id=1, source_target_pairs={{0,8},{8,16},{16,24},{24,0},{1,9},{9,17},{17,25},{25,1},{2,10},{10... | collective-permute-start | bytes 835592 | tf_op jit(solution)/shard_map/ppermute | solution.py:274
  154.7 32.7 %collective-permute-start.21 = (bf16[8,4,64,128]{3,2,1,0:T(8,128)(2,1)S(1)}, bf16[8,4,64,128]{3,2,1,0:T(8,128)(2,1)S(1)}, u32[]{:S(2)}, u32[]{:S(2)}) collective-permute-start(bf16[8,4,64,128]{3,2,1,0:T(8,128)(2,1)S(1)} %slice.53.refs_0_), channel_id=1, source_target_pairs={{0,32},{32,64},{64,96},{96,0},{1,33},{33,65},{65,97},{97,1},{2,34}... | collective-permute-start | bytes 1572872 | tf_op jit(solution)/shard_map/ppermute | solution.py:267
  154.8 32.6 %collective-permute-start.22 = (bf16[8,4,64,128]{3,2,1,0:T(8,128)(2,1)S(1)}, bf16[8,4,64,128]{3,2,1,0:T(8,128)(2,1)S(1)}, u32[]{:S(2)}, u32[]{:S(2)}) collective-permute-start(bf16[8,4,64,128]{3,2,1,0:T(8,128)(2,1)S(1)} %slice.53.refs_0_), channel_id=1, source_target_pairs={{0,64},{32,96},{64,0},{96,32},{1,65},{33,97},{65,1},{97,33},{2,66}... | collective-permute-start | bytes 1572872 | tf_op jit(solution)/shard_map/ppermute | solution.py:267
  160.4 27.0 %collective-permute-start.23 = (bf16[8,4,64,128]{3,2,1,0:T(8,128)(2,1)S(1)}, bf16[8,4,64,128]{3,2,1,0:T(8,128)(2,1)S(1)}, u32[]{:S(2)}, u32[]{:S(2)}) collective-permute-start(bf16[8,4,64,128]{3,2,1,0:T(8,128)(2,1)S(1)} %slice.53.refs_0_), channel_id=1, source_target_pairs={{0,96},{32,0},{64,32},{96,64},{1,97},{33,1},{65,33},{97,65},{2,98}... | collective-permute-start | bytes 1572872 | tf_op jit(solution)/shard_map/ppermute | solution.py:267
  164.5 17.8 %all-to-all-start.1 = ((bf16[8,2,64,128]{3,2,1,0:T(8,128)(2,1)}), bf16[8,2,64,128]{3,2,1,0:T(8,128)(2,1)}, u32[]{:S(2)}, u32[]{:S(2)}) async-start(bf16[8,2,64,128]{3,2,1,0:T(8,128)(2,1)} %combine.3), calls=%async_computation.1 | async-start | bytes 524288 | tf_op jit(solution)/shard_map/all_to_all | solution.py:278
  171.6 15.7 %collective-permute-start.25 = (bf16[8,2,64,128]{3,2,1,0:T(8,128)(2,1)S(1)}, bf16[8,2,64,128]{3,2,1,0:T(8,128)(2,1)}, u32[]{:S(2)}, u32[]{:S(2)}) collective-permute-start(bf16[8,2,64,128]{3,2,1,0:T(8,128)(2,1)S(1)} %slice.54.refs_4_), channel_id=1, source_target_pairs={{0,16},{8,24},{16,0},{24,8},{1,17},{9,25},{17,1},{25,9},{2,18},{10... | collective-permute-start | bytes 786440 | tf_op jit(solution)/shard_map/ppermute | solution.py:270
  176.7 10.7 %collective-permute-start.26 = (bf16[8,2,64,128]{3,2,1,0:T(8,128)(2,1)S(1)}, bf16[8,2,64,128]{3,2,1,0:T(8,128)(2,1)}, u32[]{:S(2)}, u32[]{:S(2)}) collective-permute-start(bf16[8,2,64,128]{3,2,1,0:T(8,128)(2,1)S(1)} %slice.54.refs_4_), channel_id=1, source_target_pairs={{0,24},{8,0},{16,8},{24,16},{1,25},{9,1},{17,9},{25,17},{2,26},{10... | collective-permute-start | bytes 786440 | tf_op jit(solution)/shard_map/ppermute | solution.py:270
  182.3 36.7 %all-to-all-start.3 = ((bf16[8,2,64,128]{3,2,1,0:T(8,128)(2,1)}), bf16[8,2,64,128]{3,2,1,0:T(8,128)(2,1)}, u32[]{:S(2)}, u32[]{:S(2)}) async-start(bf16[8,2,64,128]{3,2,1,0:T(8,128)(2,1)} %combine.4), calls=%async_computation.3 | async-start | bytes 524288 | tf_op jit(solution)/shard_map/all_to_all | solution.py:278
  203.4 6.7 %collective-permute-start.27 = (bf16[4,272,128]{2,1,0:T(8,128)(2,1)S(1)}, bf16[4,272,128]{2,1,0:T(8,128)(2,1)S(1)}, u32[]{:S(2)}, u32[]{:S(2)}) collective-permute-start(bf16[4,272,128]{2,1,0:T(8,128)(2,1)S(1)} %get-tuple-element.23), channel_id=1, source_target_pairs={{0,24},{8,0},{16,8},{24,16},{1,25},{9,1},{17,9},{25,17},{2,26},{10... | collective-permute-start | bytes 835592 | tf_op jit(solution)/shard_map/ppermute | solution.py:274
  205.0 10.0 %collective-permute-start.28 = (bf16[4,272,128]{2,1,0:T(8,128)(2,1)S(1)}, bf16[4,272,128]{2,1,0:T(8,128)(2,1)S(1)}, u32[]{:S(2)}, u32[]{:S(2)}) collective-permute-start(bf16[4,272,128]{2,1,0:T(8,128)(2,1)S(1)} %get-tuple-element.24), channel_id=1, source_target_pairs={{0,16},{8,24},{16,0},{24,8},{1,17},{9,25},{17,1},{25,9},{2,18},{10... | collective-permute-start | bytes 835592 | tf_op jit(solution)/shard_map/ppermute | solution.py:274
  207.6 8.6 %collective-permute-start.29 = (bf16[4,272,128]{2,1,0:T(8,128)(2,1)S(1)}, bf16[4,272,128]{2,1,0:T(8,128)(2,1)S(1)}, u32[]{:S(2)}, u32[]{:S(2)}) collective-permute-start(bf16[4,272,128]{2,1,0:T(8,128)(2,1)S(1)} %get-tuple-element.25), channel_id=1, source_target_pairs={{0,8},{8,16},{16,24},{24,0},{1,9},{9,17},{17,25},{25,1},{2,10},{10... | collective-permute-start | bytes 835592 | tf_op jit(solution)/shard_map/ppermute | solution.py:274
  (20 other events, 237.2 us)
